TPU v7x, 512 devices: a whole 4x8x8 slice. The times are simulated.
512 devices in a mesh: gx: 32 (over y, z_lo, core), gy: 16 (over x, z_hi).
Axes of the slice: x: 4, y: 8, z: 8 (z_hi: 4, z_lo: 2; z = z_hi * 2 + z_lo), core: 2. Of those that a mesh axis runs over, the one named last changes fastest.
Arguments:
- field: bfloat16 [512, 256, 4, 64], P('gx', 'gy'), may hold values from -6 to 6
- first_kernel: bfloat16 [1728, 64], replicated, may hold values from -0.21875 to 0.21875
- second_kernel: bfloat16 [1728, 64], replicated, may hold values from -0.15625 to 0.15625
- cotangent: bfloat16 [512, 256, 4, 64], P('gx', 'gy'), may hold values from -6 to 6
- samples: int32 [32, 16, 256], P('gx', 'gy'), may hold values from 0 to 1023
Outputs:
- output: bfloat16 [512, 256, 4, 64], P('gx', 'gy')
- first_update: float32 [1728, 64], replicated
- second_update: float32 [1728, 64], replicated
All inputs are finite; a program needn't handle non-finite values.
Results may differ from a plain program's by a relative error of at most 0.0034.
Values may be sent and summed in bfloat16 or wider, within the bound.
A program may use at most 64 MiB of HBM per device.

v0:
```python
import jax
import jax.numpy as jnp
from jax import lax
from jax.sharding import PartitionSpec as P

NS_ITERS = 5


def with_halo(block, sides, width):
    for axis, dim in sides:
        count = lax.axis_size(axis)
        forward = [(i, i + 1) for i in range(count - 1)]
        backward = [(target, source) for source, target in forward]
        low = lax.ppermute(
            lax.slice_in_dim(block, block.shape[dim] - width, None, axis=dim), axis, forward
        )
        high = lax.ppermute(lax.slice_in_dim(block, 0, width, axis=dim), axis, backward)
        block = jnp.concatenate([low, block, high], axis=dim)
    return block


def patches(padded, row_index, ylen, zlen):
    slab = lax.dynamic_slice_in_dim(padded, row_index, 3, 0)
    pieces = [
        slab[first, second : second + ylen, third : third + zlen, :]
        for first in range(3)
        for second in range(3)
        for third in range(3)
    ]
    return jnp.concatenate(pieces, -1).reshape(ylen * zlen, -1)


def convolve(framed, kernel):
    padded = jnp.pad(framed, ((0, 0), (0, 0), (1, 1), (0, 0)))
    xlen = framed.shape[0] - 2
    ylen = framed.shape[1] - 2
    zlen = framed.shape[2]
    width = kernel.shape[1]

    def one_row(row_index):
        return jnp.dot(
            patches(padded, row_index, ylen, zlen), kernel, preferred_element_type=jnp.float32
        )

    result = lax.map(one_row, jnp.arange(xlen, dtype=jnp.int32))
    return result.reshape(xlen, ylen, zlen, width)


def kernel_grad(framed, grads):
    padded = jnp.pad(framed, ((0, 0), (0, 0), (1, 1), (0, 0)))
    xlen, ylen, zlen, width = grads.shape

    def add_row(row_index, total):
        block = lax.dynamic_index_in_dim(grads, row_index, 0, keepdims=False).reshape(
            ylen * zlen, width
        )
        return total + jnp.dot(
            patches(padded, row_index, ylen, zlen).T, block, preferred_element_type=jnp.float32
        )

    start = jnp.zeros((27 * framed.shape[3], width), jnp.float32)
    return lax.fori_loop(0, xlen, add_row, start)


def flip_kernel(kernel, width):
    blocks = kernel.reshape(3, 3, 3, width, width)[::-1, ::-1, ::-1]
    return jnp.transpose(blocks, (0, 1, 2, 4, 3)).reshape(27 * width, width)


def newton_inverse(factor):
    width = factor.shape[0]
    identity = jnp.eye(width, dtype=jnp.float32)
    matrix = factor + 0.1 * identity
    approx = identity / jnp.sqrt(jnp.sum(matrix * matrix))
    for step in range(NS_ITERS):
        inner = 2.0 * identity - jnp.dot(matrix, approx, precision=lax.Precision.HIGHEST)
        approx = jnp.dot(approx, inner, precision=lax.Precision.HIGHEST)
    return approx


def precondition(grad, left_inv, right_inv, width):
    blocks = grad.reshape(27, width, width)
    result = jnp.einsum(
        "ab,tbc,cd->tad", left_inv, blocks, right_inv, precision=lax.Precision.HIGHEST
    )
    return result.reshape(27 * width, width)


def local_gram(values, cells, count):
    width = values.shape[3]
    picked = jnp.take(values.reshape(-1, width), cells, axis=0)
    return jnp.dot(picked.T, picked, preferred_element_type=jnp.float32) / count


def layer_inverses(inputs, outputs, cells, count):
    left_gram, right_gram = lax.psum(
        (local_gram(inputs, cells, count), local_gram(outputs, cells, count)), ("gx", "gy")
    )
    return (newton_inverse(left_gram), newton_inverse(right_gram))


def local(field, first_kernel, second_kernel, cotangent, samples):
    width = field.shape[3]
    xlen, ylen, zlen = (field.shape[0], field.shape[1], field.shape[2])
    tiles = lax.axis_size("gx") * lax.axis_size("gy")
    count = jnp.float32(tiles * samples.shape[2])
    cells = samples.reshape(-1)
    scale = 1.0 / jnp.sqrt(jnp.float32(tiles * xlen * ylen * zlen))
    framed_field = with_halo(field, (("gx", 0), ("gy", 1)), 1)
    hidden_pre = convolve(framed_field, first_kernel)
    hidden = jax.nn.silu(hidden_pre).astype(jnp.bfloat16)
    framed_hidden = with_halo(hidden, (("gx", 0), ("gy", 1)), 1)
    output = (field.astype(jnp.float32) + convolve(framed_hidden, second_kernel)).astype(
        jnp.bfloat16
    )
    framed_cotangent = with_halo(cotangent, (("gx", 0), ("gy", 1)), 1)
    second_grad = kernel_grad(framed_hidden, cotangent) * scale
    second_left, second_right = layer_inverses(hidden, cotangent, cells, count)
    back = convolve(framed_cotangent, flip_kernel(second_kernel, width))
    sigma = jax.nn.sigmoid(hidden_pre)
    delta = (back * sigma * (1.0 + hidden_pre * (1.0 - sigma))).astype(jnp.bfloat16)
    first_grad = kernel_grad(framed_field, delta) * scale
    first_left, first_right = layer_inverses(field, delta, cells, count)
    second_total, first_total = lax.psum((second_grad, first_grad), ("gx", "gy"))
    first_update = precondition(first_total, first_left, first_right, width)
    second_update = precondition(second_total, second_left, second_right, width)
    return (output, first_update, second_update)


def solution(mesh):
    placed = (P("gx", "gy", None, None), P(), P(), P("gx", "gy", None, None), P("gx", "gy", None))
    return jax.shard_map(
        local,
        mesh=mesh,
        in_specs=placed,
        out_specs=(P("gx", "gy", None, None), P(), P()),
        check_vma=False,
    )
```

profile of v0, /device:TPU:1, one launch (start us, length us, event | category | flops | bytes accessed | tf_op | source)
XLA Modules:
  0.0 836.6 jit_solution(13182387417172492346)
XLA Ops:
  8.0 5.4 collective-permute-start
  13.4 4.7 collective-permute-start.1
  18.9 1.9 collective-permute-start.8
  20.8 2.4 collective-permute-start.9
  24.6 1.7 gather_fusion.3
  29.3 1.7 rev.3
  31.4 4.3 collective-permute-start.2
  35.7 1.3 collective-permute-start.3
  37.9 7.3 collective-permute-start.10
  45.2 1.3 collective-permute-start.11
  47.0 75.0 %while.58 = (s32[]{:T(128)}, f32[16,64,64]{2,1,0:T(8,128)S(1)}, s32[16]{0:T(128)S(1)}, bf16[18,18,6,64]{3,2,1,0:T(8,128)(2,1)S(1)}, bf16[1728,64]{0,1:T(8,128)(2...) while((s32[]{:T(128)}, f32[16,64,64]{2,1,0:T(8,128)S(1)}, s32[16]{0:T(128)S(1)}, ...), condition=%wide.region_1.2_spmd, body=%wide.region_0.1_spmd.sunk | while | flops 14155785 | bytes 1376475 | solution.py:45
  122.0 1.5 select_maximum_fusion
  125.0 96.4 %while.60 = (s32[]{:T(128)}, f32[16,64,64]{2,1,0:T(8,128)}, s32[16]{0:T(128)}, bf16[18,18,6,64]{3,2,1,0:T(8,128)(2,1)S(1)}, bf16[1728,64]{1,0:T(8,128)(2,1)S(1)}...) while((s32[]{:T(128)}, f32[16,64,64]{2,1,0:T(8,128)}, s32[16]{0:T(128)}, ...), condition=%wide.region_5.6_spmd, body=%wide.region_4.5_spmd.sunk | while | flops 14155785 | bytes 1360599 | solution.py:45
  125.0 1.2 dynamic_slice.59
  129.1 1.1 concatenate.385
  131.0 1.2 dynamic_slice.59
  135.1 1.1 concatenate.385
  137.0 1.2 dynamic_slice.59
  141.2 1.1 concatenate.385
  143.1 1.2 dynamic_slice.59
  147.2 1.1 concatenate.385
  149.1 1.2 dynamic_slice.59
  153.2 1.1 concatenate.385
  155.1 1.2 dynamic_slice.59
  159.2 1.1 concatenate.385
  161.1 1.2 dynamic_slice.59
  165.2 1.1 concatenate.385
  167.2 1.2 dynamic_slice.59
  171.3 1.1 concatenate.385
  173.2 1.2 dynamic_slice.59
  177.3 1.1 concatenate.385
  179.2 1.2 dynamic_slice.59
  183.3 1.1 concatenate.385
  185.2 1.2 dynamic_slice.59
  189.3 1.1 concatenate.385
  191.3 1.2 dynamic_slice.59
  195.4 1.1 concatenate.385
  197.3 1.2 dynamic_slice.59
  201.4 1.1 concatenate.385
  203.3 1.2 dynamic_slice.59
  207.4 1.1 concatenate.385
  209.3 1.2 dynamic_slice.59
  213.4 1.1 concatenate.385
  215.3 1.2 dynamic_slice.59
  219.4 1.1 concatenate.385
  221.4 1.5 fusion.20
  223.8 1.2 multiply_convert_fusion
  225.0 4.2 collective-permute-start.4
  229.2 1.9 collective-permute-start.5
  231.2 25.0 %while.61 = (s32[]{:T(128)}, f32[1728,64]{0,1:T(8,128)S(1)}, bf16[18,18,6,64]{3,2,1,0:T(8,128)(2,1)S(1)}, bf16[16,16,4,64]{3,2,1,0:T(4,128)(2,1)}, s32[]{:T(128)}, /*index=5*/s32[]{}, s32[]{:T(128)}, s32[]{}) while((s32[]{:T(128)}, f32[1728,64]{0,1:T(8,128)S(1)}, bf16[18,18,6,64]{3,2,1,0:T(8,128)(2,1)S(1)}, ...), condition=%wide.region_7.8_spmd.clone, body=%wide.region_6.7_spmd.clone.sunk | while | flops 14376967 | bytes 2015395 | solution.py:62
  258.0 5.8 collective-permute-start.6
  263.8 1.3 collective-permute-start.7
  266.4 1.5 copy.15
  268.1 2.6 collective-permute-done.7
  271.2 25.0 %while.62 = (s32[]{:T(128)}, f32[1728,64]{0,1:T(8,128)S(1)}, bf16[18,18,6,64]{3,2,1,0:T(8,128)(2,1)S(1)}, bf16[16,16,4,64]{3,2,1,0:T(4,128)(2,1)}, s32[]{:T(128)}, /*index=5*/s32[]{}, s32[]{:T(128)}, s32[]{}) while((s32[]{:T(128)}, f32[1728,64]{0,1:T(8,128)S(1)}, bf16[18,18,6,64]{3,2,1,0:T(8,128)(2,1)S(1)}, ...), condition=%wide.region_14.16_spmd.clone, body=%wide.region_13.15_spmd.clone.sunk | while | flops 14376967 | bytes 2015395 | solution.py:62
  296.4 51.7 %while.59 = (s32[]{:T(128)}, f32[16,64,64]{2,1,0:T(8,128)S(1)}, s32[16]{0:T(128)S(1)}, bf16[18,18,6,64]{3,2,1,0:T(8,128)(2,1)S(1)}, bf16[1728,64]{0,1:T(8,128)(2...) while((s32[]{:T(128)}, f32[16,64,64]{2,1,0:T(8,128)S(1)}, s32[16]{0:T(128)S(1)}, ...), condition=%wide.region_3.4_spmd, body=%wide.region_2.3_spmd.sunk | while | flops 14155785 | bytes 1376475 | solution.py:45
  349.4 1.5 copy.17
  350.9 191.8 %all-reduce.8.cloned.1.call-done = (f32[64,64]{1,0:T(8,128)}, f32[64,64]{1,0:T(8,128)}, f32[64,64]{1,0:T(8,128)}, f32[64,64]{1,0:T(8,128)}) async-done(((f32[64,64]{1,0:T(8,128)}, f32[64,64]{1,0:T(8,128)}, f32[64,64]{1,0:T(8,128)}, f32[64,64]{1,0:T(8,128)}), (f32[64,64]{1,0:T(8,128)}, f32[64,64]{1,0:T(8,128)}, f32[64,64]{1,0:T(8,128)}, f32[64,64]{1,0:T(8,128)})) %all-reduce.8.cloned.1.call-update) | async-done | bytes 65552 | tf_op jit(solution)/shard_map/psum | solution.py:96
  542.7 1.4 multiply_reduce_fusion
  558.9 261.1 %all-reduce.10.cloned.1.call-done = (f32[27,64,64]{1,2,0:T(8,128)}, f32[27,64,64]{1,2,0:T(8,128)}) async-done(((f32[27,64,64]{1,2,0:T(8,128)}, f32[27,64,64]{1,2,0:T(8,128)}), (f32[27,64,64]{1,2,0:T(8,128)}, f32[27,64,64]{1,2,0:T(8,128)})) %all-reduce.10.cloned.1.call-update) | async-done | bytes 884752 | tf_op jit(solution)/shard_map/psum | solution.py:124
  820.0 3.5 fusion.125
  824.4 1.1 copy.20
  825.5 2.4 fusion.117
  828.7 1.1 copy.19
  (387 shorter events, 169.4 us)
Async XLA Ops:
  7.2 19.2 %copy-start.5 = (bf16[16,16,4,64]{3,2,1,0:T(4,128)(2,1)S(1)}, bf16[16,16,4,64]{3,2,1,0:T(4,128)(2,1)}, u32[]{:S(2)}) copy-start(bf16[16,16,4,64]{3,2,1,0:T(4,128)(2,1)} %param.17) | copy-start | bytes 393220
  7.2 21.8 %copy-start = (bf16[1728,64]{0,1:T(8,128)(2,1)S(1)}, bf16[1728,64]{0,1:T(8,128)(2,1)}, u32[]{:S(2)}) copy-start(bf16[1728,64]{0,1:T(8,128)(2,1)} %param.19) | copy-start | bytes 663556
  7.2 535.5 %all-reduce.8.cloned.1.call-start = ((), (), s32[]{:S(2)}) async-start(), calls=%async_computation | async-start | bytes 262144 | tf_op jit(solution)/shard_map/psum | solution.py:96
  8.0 23.1 %collective-permute-start = (bf16[1,16,4,64]{3,2,1,0:T(4,128)(2,1)S(1)}, bf16[1,16,4,64]{3,2,1,0:T(4,128)(2,1)S(1)}, u32[]{:S(2)}, u32[]{:S(2)}) collective-permute-start(bf16[1,16,4,64]{3,2,1,0:T(4,128)(2,1)S(1)} %get-tuple-element.496), channel_id=1, source_target_pairs={{0,16},{16,32},{32,48},{48,64},{64,80},{80,96},{96,112},{112,128},... | collective-permute-start | bytes 24584 | tf_op jit(solution)/shard_map/ppermute | solution.py:14
  13.4 17.9 %collective-permute-start.1 = (bf16[1,16,4,64]{3,2,1,0:T(4,128)(2,1)S(1)}, bf16[1,16,4,64]{3,2,1,0:T(4,128)(2,1)S(1)}, u32[]{:S(2)}, u32[]{:S(2)}) collective-permute-start(bf16[1,16,4,64]{3,2,1,0:T(4,128)(2,1)S(1)} %get-tuple-element.495), channel_id=1, source_target_pairs={{16,0},{32,16},{48,32},{64,48},{80,64},{96,80},{112,96},{128,112},... | collective-permute-start | bytes 24584 | tf_op jit(solution)/shard_map/ppermute | solution.py:17
  18.9 18.1 %collective-permute-start.8 = (bf16[1,16,4,64]{3,2,1,0:T(4,128)(2,1)S(1)}, bf16[1,16,4,64]{3,2,1,0:T(4,128)(2,1)S(1)}, u32[]{:S(2)}, u32[]{:S(2)}) collective-permute-start(bf16[1,16,4,64]{3,2,1,0:T(4,128)(2,1)S(1)} %get-tuple-element.492), channel_id=1, source_target_pairs={{0,16},{16,32},{32,48},{48,64},{64,80},{80,96},{96,112},{112,128},... | collective-permute-start | bytes 24584 | tf_op jit(solution)/shard_map/ppermute | solution.py:14
  20.8 16.3 %collective-permute-start.9 = (bf16[1,16,4,64]{3,2,1,0:T(4,128)(2,1)S(1)}, bf16[1,16,4,64]{3,2,1,0:T(4,128)(2,1)S(1)}, u32[]{:S(2)}, u32[]{:S(2)}) collective-permute-start(bf16[1,16,4,64]{3,2,1,0:T(4,128)(2,1)S(1)} %get-tuple-element.491), channel_id=1, source_target_pairs={{16,0},{32,16},{48,32},{64,48},{80,64},{96,80},{112,96},{128,112},... | collective-permute-start | bytes 24584 | tf_op jit(solution)/shard_map/ppermute | solution.py:17
  24.6 4.7 copy-start.15
  24.6 4.4 copy-start.13
  31.0 6.0 copy-start.7
  31.4 15.1 %collective-permute-start.2 = (bf16[18,1,4,64]{3,2,1,0:T(4,128)(2,1)S(1)}, bf16[18,1,4,64]{3,2,1,0:T(4,128)(2,1)S(1)}, u32[]{:S(2)}, u32[]{:S(2)}) collective-permute-start(bf16[18,1,4,64]{3,2,1,0:T(4,128)(2,1)S(1)} %get-tuple-element.489), channel_id=1, source_target_pairs={{0,1},{1,2},{2,3},{3,4},{4,5},{5,6},{6,7},{7,8},{8,9},{9,10},{10,1... | collective-permute-start | bytes 27656 | tf_op jit(solution)/shard_map/ppermute | solution.py:14
  35.7 10.9 %collective-permute-start.3 = (bf16[18,1,4,64]{3,2,1,0:T(4,128)(2,1)S(1)}, bf16[18,1,4,64]{3,2,1,0:T(4,128)(2,1)S(1)}, u32[]{:S(2)}, u32[]{:S(2)}) collective-permute-start(bf16[18,1,4,64]{3,2,1,0:T(4,128)(2,1)S(1)} %get-tuple-element.490), channel_id=1, source_target_pairs={{1,0},{2,1},{3,2},{4,3},{5,4},{6,5},{7,6},{8,7},{9,8},{10,9},{11,1... | collective-permute-start | bytes 27656 | tf_op jit(solution)/shard_map/ppermute | solution.py:17
  37.0 10.0 %copy-start.1 = (bf16[1728,64]{0,1:T(8,128)(2,1)S(1)}, bf16[1728,64]{0,1:T(8,128)(2,1)}, u32[]{:S(2)}) copy-start(bf16[1728,64]{0,1:T(8,128)(2,1)} %param.18) | copy-start | bytes 663556
  37.2 9.7 %copy-start.12 = (bf16[18,16,4,64]{3,2,1,0:T(4,128)(2,1)}, bf16[18,16,4,64]{3,2,1,0:T(4,128)(2,1)S(1)}, u32[]{:S(2)}) copy-start(bf16[18,16,4,64]{3,2,1,0:T(4,128)(2,1)S(1)} %constant_dynamic-update-slice_fusion.3) | copy-start | bytes 442372
  37.9 84.1 %collective-permute-start.10 = (bf16[18,1,4,64]{3,2,1,0:T(4,128)(2,1)}, bf16[18,1,4,64]{3,2,1,0:T(4,128)(2,1)}, u32[]{:S(2)}, u32[]{:S(2)}) collective-permute-start(bf16[18,1,4,64]{3,2,1,0:T(4,128)(2,1)} %get-tuple-element.485), channel_id=1, source_target_pairs={{0,1},{1,2},{2,3},{3,4},{4,5},{5,6},{6,7},{7,8},{8,9},{9,10},{10,1... | collective-permute-start | bytes 27656 | tf_op jit(solution)/shard_map/ppermute | solution.py:14
  45.2 76.8 %collective-permute-start.11 = (bf16[18,1,4,64]{3,2,1,0:T(4,128)(2,1)}, bf16[18,1,4,64]{3,2,1,0:T(4,128)(2,1)}, u32[]{:S(2)}, u32[]{:S(2)}) collective-permute-start(bf16[18,1,4,64]{3,2,1,0:T(4,128)(2,1)} %get-tuple-element.486), channel_id=1, source_target_pairs={{1,0},{2,1},{3,2},{4,3},{5,4},{6,5},{7,6},{8,7},{9,8},{10,9},{11,1... | collective-permute-start | bytes 27656 | tf_op jit(solution)/shard_map/ppermute | solution.py:17
  122.0 3.0 copy-start.2
  221.4 1.6 copy-start.14
  221.4 2.4 copy-start.3
  221.4 2.4 copy-start.4
  225.0 33.0 %collective-permute-start.4 = (bf16[1,16,4,64]{3,2,1,0:T(4,128)(2,1)S(1)}, bf16[1,16,4,64]{3,2,1,0:T(4,128)(2,1)S(1)}, u32[]{:S(2)}, u32[]{:S(2)}) collective-permute-start(bf16[1,16,4,64]{3,2,1,0:T(4,128)(2,1)S(1)} %get-tuple-element.493), channel_id=1, source_target_pairs={{0,16},{16,32},{32,48},{48,64},{64,80},{80,96},{96,112},{112,128},... | collective-permute-start | bytes 24584 | tf_op jit(solution)/shard_map/ppermute | solution.py:14
  229.2 28.8 %collective-permute-start.5 = (bf16[1,16,4,64]{3,2,1,0:T(4,128)(2,1)S(1)}, bf16[1,16,4,64]{3,2,1,0:T(4,128)(2,1)S(1)}, u32[]{:S(2)}, u32[]{:S(2)}) collective-permute-start(bf16[1,16,4,64]{3,2,1,0:T(4,128)(2,1)S(1)} %get-tuple-element.494), channel_id=1, source_target_pairs={{16,0},{32,16},{48,32},{64,48},{80,64},{96,80},{112,96},{128,112},... | collective-permute-start | bytes 24584 | tf_op jit(solution)/shard_map/ppermute | solution.py:17
  231.1 25.1 %copy-start.16 = (pred[256]{0:T(512)(128)(4,1)S(1)}, pred[256]{0:T(512)(128)(4,1)}, u32[]{:S(2)}) copy-start(pred[256]{0:T(512)(128)(4,1)} %copy-done.15) | copy-start | bytes 772
  258.0 10.1 %collective-permute-start.6 = (bf16[18,1,4,64]{3,2,1,0:T(4,128)(2,1)S(1)}, bf16[18,1,4,64]{3,2,1,0:T(4,128)(2,1)S(1)}, u32[]{:S(2)}, u32[]{:S(2)}) collective-permute-start(bf16[18,1,4,64]{3,2,1,0:T(4,128)(2,1)S(1)} %get-tuple-element.487), channel_id=1, source_target_pairs={{0,1},{1,2},{2,3},{3,4},{4,5},{5,6},{6,7},{7,8},{8,9},{9,10},{10,1... | collective-permute-start | bytes 27656 | tf_op jit(solution)/shard_map/ppermute | solution.py:14
  263.8 6.9 collective-permute-start.7
  267.9 552.1 %all-reduce.10.cloned.1.call-start = ((), (), s32[]{:S(2)}) async-start(), calls=%async_computation.1 | async-start | bytes 3538944 | tf_op jit(solution)/shard_map/psum | solution.py:124
  296.3 51.8 %copy-start.6 = (bf16[16,16,4,64]{3,2,1,0:T(4,128)(2,1)S(1)}, bf16[16,16,4,64]{3,2,1,0:T(4,128)(2,1)}, u32[]{:S(2)}) copy-start(bf16[16,16,4,64]{3,2,1,0:T(4,128)(2,1)} %param.17) | copy-start | bytes 393220
  542.7 9.4 %copy-start.11 = (f32[64,64]{1,0:T(8,128)S(1)}, f32[64,64]{1,0:T(8,128)}, u32[]{:S(2)}) copy-start(f32[64,64]{1,0:T(8,128)} %get-tuple-element.340) | copy-start | bytes 49156
  542.7 10.8 %copy-start.9 = (f32[64,64]{1,0:T(8,128)S(1)}, f32[64,64]{1,0:T(8,128)}, u32[]{:S(2)}) copy-start(f32[64,64]{1,0:T(8,128)} %get-tuple-element.338) | copy-start | bytes 49156
  542.7 10.8 %copy-start.10 = (f32[64,64]{1,0:T(8,128)S(1)}, f32[64,64]{1,0:T(8,128)}, u32[]{:S(2)}) copy-start(f32[64,64]{1,0:T(8,128)} %get-tuple-element.339) | copy-start | bytes 49156
  824.3 1.2 copy-start.8
Sparse Core Ops, SparseCore 0:
  268.0 274.6 all-reduce.7
  548.6 271.3 all-reduce.9
where the time goes:
time: 845 us; the launch traced here: 837 us
  waiting for transfers between devices  456 us (54%)
  local copies, waits for them, and re-layouts  165 us (20%)
  loops' own time  95.5 us (11%)
  matrix products  51.6 us (6%)
  starting transfers between devices  42.1 us (5%)
  between operations  17.7 us (2%)
  other arithmetic  9.56 us (1%)
    psum x1, waiting for transfers between devices, local(): lax.psum((second_grad, first_grad), ('gx', 'gy'))  261 us
    psum x1, waiting for transfers between devices, layer_inverses(): lax.psum((local_gram(inputs, cells, count), local_gram(outputs, cells, co...  192 us
    another operation x3, loops' own time, convolve(): result = lax.map(one_row, jnp.arange(xlen, dtype=jnp.int32))  94.1 us
    slice x80, local copies, waits for them, and re-layouts, patches(): slab[first, second:second + ylen, third:third + zlen, :]  68.1 us
    concatenate x80, local copies, waits for them, and re-layouts, patches(): return jnp.concatenate(pieces, -1).reshape(ylen * zlen, -1)  41.4 us
    dynamic_slice x48, local copies, waits for them, and re-layouts, convolve(): result = lax.map(one_row, jnp.arange(xlen, dtype=jnp.int32))  38.6 us
    ppermute x6, starting transfers between devices, with_halo(): lax.ppermute(lax.slice_in_dim(block, block.shape[dim] - width, None, axis...  28.9 us
    dot_general x48, matrix products, one_row(): jnp.dot(patches(padded, row_index, ylen, zlen), kernel, preferred_element...  19.9 us
  transfers between devices with their start and end apart: 14, of which 3 were waited for; matrix products, arithmetic and copies ran while one was open for 17% of the time, Pallas kernels for 0%

commit v1 on v0

--- a/solution.py
+++ b/solution.py
@@ -94,7 +94,7 @@
 
 def layer_inverses(inputs, outputs, cells, count):
     left_gram, right_gram = lax.psum(
-        (local_gram(inputs, cells, count), local_gram(outputs, cells, count)), ("gx", "gy")
+        lax.psum((local_gram(inputs, cells, count), local_gram(outputs, cells, count)), "gy"), "gx"
     )
     return (newton_inverse(left_gram), newton_inverse(right_gram))
 

time: 845 us -> 966 us (1.14)
  waiting for transfers between devices: 456 us -> 577 us
    psum x0 -> x1, waiting for transfers between devices: none -> 216 us  [layer_inverses(): lax.psum(lax.psum((local_gram(inputs, cells, count), local_gram(outputs,...]
    psum x1, waiting for transfers between devices: 192 us -> 90.6 us  [layer_inverses(): lax.psum((local_gram(inputs, cells, count), local_gram(outputs, cells, co...]
  transfers between devices with their start and end apart: 14 -> 15, of which waited for: 3 -> 4; matrix products, arithmetic and copies ran while one was open for 17% -> 15% of each run, Pallas kernels for 0% -> 0%
where the time goes in v1:
time: 966 us; the launch traced here: 958 us
  waiting for transfers between devices  577 us (60%)
  local copies, waits for them, and re-layouts  168 us (17%)
  loops' own time  91.4 us (9%)
  matrix products  51.8 us (5%)
  starting transfers between devices  42.1 us (4%)
  between operations  17.4 us (2%)
  other arithmetic  10.1 us (1%)
    psum x1, waiting for transfers between devices, local(): lax.psum((second_grad, first_grad), ('gx', 'gy'))  267 us
    psum x1, waiting for transfers between devices, layer_inverses(): lax.psum(lax.psum((local_gram(inputs, cells, count), local_gram(outputs,...  216 us
    psum x1, waiting for transfers between devices, layer_inverses(): lax.psum((local_gram(inputs, cells, count), local_gram(outputs, cells, co...  90.6 us
    another operation x3, loops' own time, convolve(): result = lax.map(one_row, jnp.arange(xlen, dtype=jnp.int32))  90 us
    slice x80, local copies, waits for them, and re-layouts, patches(): slab[first, second:second + ylen, third:third + zlen, :]  69.4 us
    concatenate x80, local copies, waits for them, and re-layouts, patches(): return jnp.concatenate(pieces, -1).reshape(ylen * zlen, -1)  43.1 us
    dynamic_slice x48, local copies, waits for them, and re-layouts, convolve(): result = lax.map(one_row, jnp.arange(xlen, dtype=jnp.int32))  38.1 us
    ppermute x6, starting transfers between devices, with_halo(): lax.ppermute(lax.slice_in_dim(block, block.shape[dim] - width, None, axis...  28.9 us
  transfers between devices with their start and end apart: 15, of which 4 were waited for; matrix products, arithmetic and copies ran while one was open for 15% of the time, Pallas kernels for 0%

profile of v1, /device:TPU:1, one launch (start us, length us, event | category | flops | bytes accessed | tf_op | source)
XLA Modules:
  0.0 957.7 jit_solution(17429839297407273004)
XLA Ops:
  8.0 5.4 collective-permute-start
  13.4 4.7 collective-permute-start.1
  18.9 1.9 collective-permute-start.8
  20.8 2.4 collective-permute-start.9
  24.6 1.7 gather_fusion.3
  29.3 1.7 rev.3
  31.4 4.3 collective-permute-start.2
  35.6 1.3 collective-permute-start.3
  37.8 7.3 collective-permute-start.10
  45.2 1.3 collective-permute-start.11
  47.0 72.8 %while.58 = (s32[]{:T(128)}, f32[16,64,64]{2,1,0:T(8,128)S(1)}, s32[16]{0:T(128)S(1)}, bf16[18,18,6,64]{3,2,1,0:T(8,128)(2,1)S(1)}, bf16[1728,64]{0,1:T(8,128)(2...) while((s32[]{:T(128)}, f32[16,64,64]{2,1,0:T(8,128)S(1)}, s32[16]{0:T(128)S(1)}, ...), condition=%wide.region_1.2_spmd, body=%wide.region_0.1_spmd.sunk | while | flops 14155785 | bytes 1376475 | solution.py:45
  50.2 1.1 concatenate.383
  54.7 1.1 concatenate.383
  59.3 1.1 concatenate.383
  63.8 1.1 concatenate.383
  68.4 1.1 concatenate.383
  72.9 1.1 concatenate.383
  77.5 1.1 concatenate.383
  82.0 1.1 concatenate.383
  86.6 1.1 concatenate.383
  91.1 1.1 concatenate.383
  95.7 1.1 concatenate.383
  100.3 1.1 concatenate.383
  104.8 1.1 concatenate.383
  109.4 1.1 concatenate.383
  113.9 1.1 concatenate.383
  118.5 1.1 concatenate.383
  120.6 1.4 select_maximum_fusion
  123.4 96.7 %while.60 = (s32[]{:T(128)}, f32[16,64,64]{2,1,0:T(8,128)}, s32[16]{0:T(128)}, bf16[18,18,6,64]{3,2,1,0:T(8,128)(2,1)S(1)}, bf16[1728,64]{1,0:T(8,128)(2,1)S(1)}...) while((s32[]{:T(128)}, f32[16,64,64]{2,1,0:T(8,128)}, s32[16]{0:T(128)}, ...), condition=%wide.region_5.6_spmd, body=%wide.region_4.5_spmd.sunk | while | flops 14155785 | bytes 1360599 | solution.py:45
  123.4 1.2 dynamic_slice.59
  129.4 1.2 dynamic_slice.59
  135.5 1.2 dynamic_slice.59
  141.5 1.2 dynamic_slice.59
  147.6 1.2 dynamic_slice.59
  151.7 1.1 concatenate.385
  153.6 1.2 dynamic_slice.59
  159.7 1.2 dynamic_slice.59
  165.7 1.2 dynamic_slice.59
  171.8 1.2 dynamic_slice.59
  177.8 1.2 dynamic_slice.59
  183.8 1.2 dynamic_slice.59
  189.9 1.2 dynamic_slice.59
  195.9 1.2 dynamic_slice.59
  202.0 1.2 dynamic_slice.59
  208.0 1.2 dynamic_slice.59
  214.1 1.2 dynamic_slice.59
  220.1 2.2 fusion.20
  223.2 1.2 multiply_convert_fusion
  224.4 4.2 collective-permute-start.4
  228.7 1.9 collective-permute-start.5
  230.6 25.0 %while.61 = (s32[]{:T(128)}, f32[1728,64]{0,1:T(8,128)S(1)}, bf16[18,18,6,64]{3,2,1,0:T(8,128)(2,1)S(1)}, bf16[16,16,4,64]{3,2,1,0:T(4,128)(2,1)}, s32[]{:T(128)}, /*index=5*/s32[]{}, s32[]{:T(128)}, s32[]{}) while((s32[]{:T(128)}, f32[1728,64]{0,1:T(8,128)S(1)}, bf16[18,18,6,64]{3,2,1,0:T(8,128)(2,1)S(1)}, ...), condition=%wide.region_7.8_spmd.clone, body=%wide.region_6.7_spmd.clone.sunk | while | flops 14376967 | bytes 2015395 | solution.py:62
  257.5 5.8 collective-permute-start.6
  263.3 1.3 collective-permute-start.7
  265.9 1.4 copy.15
  267.4 2.8 collective-permute-done.7
  270.7 25.1 %while.62 = (s32[]{:T(128)}, f32[1728,64]{0,1:T(8,128)S(1)}, bf16[18,18,6,64]{3,2,1,0:T(8,128)(2,1)S(1)}, bf16[16,16,4,64]{3,2,1,0:T(4,128)(2,1)}, s32[]{:T(128)}, /*index=5*/s32[]{}, s32[]{:T(128)}, s32[]{}) while((s32[]{:T(128)}, f32[1728,64]{0,1:T(8,128)S(1)}, bf16[18,18,6,64]{3,2,1,0:T(8,128)(2,1)S(1)}, ...), condition=%wide.region_16.18_spmd.clone, body=%wide.region_15.17_spmd.clone.sunk | while | flops 14376967 | bytes 2015395 | solution.py:62
  295.8 52.1 %while.59 = (s32[]{:T(128)}, f32[16,64,64]{2,1,0:T(8,128)S(1)}, s32[16]{0:T(128)S(1)}, bf16[18,18,6,64]{3,2,1,0:T(8,128)(2,1)S(1)}, bf16[1728,64]{0,1:T(8,128)(2...) while((s32[]{:T(128)}, f32[16,64,64]{2,1,0:T(8,128)S(1)}, s32[16]{0:T(128)S(1)}, ...), condition=%wide.region_3.4_spmd, body=%wide.region_2.3_spmd.sunk | while | flops 14155785 | bytes 1376475 | solution.py:45
  348.0 90.6 %all-reduce.14.cloned.1.call-done = (f32[64,64]{1,0:T(8,128)}, f32[64,64]{1,0:T(8,128)}, f32[64,64]{1,0:T(8,128)}, f32[64,64]{1,0:T(8,128)}) async-done(((f32[64,64]{1,0:T(8,128)}, f32[64,64]{1,0:T(8,128)}, f32[64,64]{1,0:T(8,128)}, f32[64,64]{1,0:T(8,128)}), (f32[64,64]{1,0:T(8,128)}, f32[64,64]{1,0:T(8,128)}, f32[64,64]{1,0:T(8,128)}, f32[64,64]{1,0:T(8,128)})) %all-reduce.14.cloned.1.call-update) | async-done | bytes 65552 | tf_op jit(solution)/shard_map/psum | solution.py:97
  440.1 1.5 copy.17
  441.6 216.4 %all-reduce.12.cloned.1.call-done = (f32[64,64]{1,0:T(8,128)}, f32[64,64]{1,0:T(8,128)}, f32[64,64]{1,0:T(8,128)}, f32[64,64]{1,0:T(8,128)}) async-done(((f32[64,64]{1,0:T(8,128)}, f32[64,64]{1,0:T(8,128)}, f32[64,64]{1,0:T(8,128)}, f32[64,64]{1,0:T(8,128)}), (f32[64,64]{1,0:T(8,128)}, f32[64,64]{1,0:T(8,128)}, f32[64,64]{1,0:T(8,128)}, f32[64,64]{1,0:T(8,128)})) %all-reduce.12.cloned.1.call-update) | async-done | bytes 65552 | tf_op jit(solution)/shard_map/psum | solution.py:96
  658.0 1.4 multiply_reduce_fusion
  674.2 267.2 %all-reduce.10.cloned.1.call-done = (f32[27,64,64]{1,2,0:T(8,128)}, f32[27,64,64]{1,2,0:T(8,128)}) async-done(((f32[27,64,64]{1,2,0:T(8,128)}, f32[27,64,64]{1,2,0:T(8,128)}), (f32[27,64,64]{1,2,0:T(8,128)}, f32[27,64,64]{1,2,0:T(8,128)})) %all-reduce.10.cloned.1.call-update) | async-done | bytes 884752 | tf_op jit(solution)/shard_map/psum | solution.py:124
  941.4 3.5 fusion.125
  946.9 2.4 fusion.117
  (390 shorter events, 173.1 us)
Async XLA Ops:
  7.2 19.2 %copy-start.5 = (bf16[16,16,4,64]{3,2,1,0:T(4,128)(2,1)S(1)}, bf16[16,16,4,64]{3,2,1,0:T(4,128)(2,1)}, u32[]{:S(2)}) copy-start(bf16[16,16,4,64]{3,2,1,0:T(4,128)(2,1)} %param.17) | copy-start | bytes 393220
  7.2 21.8 %copy-start = (bf16[1728,64]{0,1:T(8,128)(2,1)S(1)}, bf16[1728,64]{0,1:T(8,128)(2,1)}, u32[]{:S(2)}) copy-start(bf16[1728,64]{0,1:T(8,128)(2,1)} %param.19) | copy-start | bytes 663556
  7.2 431.4 %all-reduce.14.cloned.1.call-start = ((), (), s32[]{:S(2)}) async-start(), calls=%async_computation.2 | async-start | bytes 262144 | tf_op jit(solution)/shard_map/psum | solution.py:97
  8.0 23.1 %collective-permute-start = (bf16[1,16,4,64]{3,2,1,0:T(4,128)(2,1)S(1)}, bf16[1,16,4,64]{3,2,1,0:T(4,128)(2,1)S(1)}, u32[]{:S(2)}, u32[]{:S(2)}) collective-permute-start(bf16[1,16,4,64]{3,2,1,0:T(4,128)(2,1)S(1)} %get-tuple-element.500), channel_id=1, source_target_pairs={{0,16},{16,32},{32,48},{48,64},{64,80},{80,96},{96,112},{112,128},... | collective-permute-start | bytes 24584 | tf_op jit(solution)/shard_map/ppermute | solution.py:14
  13.4 17.9 %collective-permute-start.1 = (bf16[1,16,4,64]{3,2,1,0:T(4,128)(2,1)S(1)}, bf16[1,16,4,64]{3,2,1,0:T(4,128)(2,1)S(1)}, u32[]{:S(2)}, u32[]{:S(2)}) collective-permute-start(bf16[1,16,4,64]{3,2,1,0:T(4,128)(2,1)S(1)} %get-tuple-element.499), channel_id=1, source_target_pairs={{16,0},{32,16},{48,32},{64,48},{80,64},{96,80},{112,96},{128,112},... | collective-permute-start | bytes 24584 | tf_op jit(solution)/shard_map/ppermute | solution.py:17
  18.9 18.1 %collective-permute-start.8 = (bf16[1,16,4,64]{3,2,1,0:T(4,128)(2,1)S(1)}, bf16[1,16,4,64]{3,2,1,0:T(4,128)(2,1)S(1)}, u32[]{:S(2)}, u32[]{:S(2)}) collective-permute-start(bf16[1,16,4,64]{3,2,1,0:T(4,128)(2,1)S(1)} %get-tuple-element.496), channel_id=1, source_target_pairs={{0,16},{16,32},{32,48},{48,64},{64,80},{80,96},{96,112},{112,128},... | collective-permute-start | bytes 24584 | tf_op jit(solution)/shard_map/ppermute | solution.py:14
  20.8 16.3 %collective-permute-start.9 = (bf16[1,16,4,64]{3,2,1,0:T(4,128)(2,1)S(1)}, bf16[1,16,4,64]{3,2,1,0:T(4,128)(2,1)S(1)}, u32[]{:S(2)}, u32[]{:S(2)}) collective-permute-start(bf16[1,16,4,64]{3,2,1,0:T(4,128)(2,1)S(1)} %get-tuple-element.495), channel_id=1, source_target_pairs={{16,0},{32,16},{48,32},{64,48},{80,64},{96,80},{112,96},{128,112},... | collective-permute-start | bytes 24584 | tf_op jit(solution)/shard_map/ppermute | solution.py:17
  24.6 4.7 copy-start.15
  24.6 4.3 copy-start.13
  31.0 6.0 copy-start.6
  31.4 15.1 %collective-permute-start.2 = (bf16[18,1,4,64]{3,2,1,0:T(4,128)(2,1)S(1)}, bf16[18,1,4,64]{3,2,1,0:T(4,128)(2,1)S(1)}, u32[]{:S(2)}, u32[]{:S(2)}) collective-permute-start(bf16[18,1,4,64]{3,2,1,0:T(4,128)(2,1)S(1)} %get-tuple-element.493), channel_id=1, source_target_pairs={{0,1},{1,2},{2,3},{3,4},{4,5},{5,6},{6,7},{7,8},{8,9},{9,10},{10,1... | collective-permute-start | bytes 27656 | tf_op jit(solution)/shard_map/ppermute | solution.py:14
  35.6 10.8 %collective-permute-start.3 = (bf16[18,1,4,64]{3,2,1,0:T(4,128)(2,1)S(1)}, bf16[18,1,4,64]{3,2,1,0:T(4,128)(2,1)S(1)}, u32[]{:S(2)}, u32[]{:S(2)}) collective-permute-start(bf16[18,1,4,64]{3,2,1,0:T(4,128)(2,1)S(1)} %get-tuple-element.494), channel_id=1, source_target_pairs={{1,0},{2,1},{3,2},{4,3},{5,4},{6,5},{7,6},{8,7},{9,8},{10,9},{11,1... | collective-permute-start | bytes 27656 | tf_op jit(solution)/shard_map/ppermute | solution.py:17
  37.0 10.0 %copy-start.1 = (bf16[1728,64]{0,1:T(8,128)(2,1)S(1)}, bf16[1728,64]{0,1:T(8,128)(2,1)}, u32[]{:S(2)}) copy-start(bf16[1728,64]{0,1:T(8,128)(2,1)} %param.18) | copy-start | bytes 663556
  37.2 9.3 copy-start.12
  37.8 82.0 %collective-permute-start.10 = (bf16[18,1,4,64]{3,2,1,0:T(4,128)(2,1)}, bf16[18,1,4,64]{3,2,1,0:T(4,128)(2,1)}, u32[]{:S(2)}, u32[]{:S(2)}) collective-permute-start(bf16[18,1,4,64]{3,2,1,0:T(4,128)(2,1)} %get-tuple-element.489), channel_id=1, source_target_pairs={{0,1},{1,2},{2,3},{3,4},{4,5},{5,6},{6,7},{7,8},{8,9},{9,10},{10,1... | collective-permute-start | bytes 27656 | tf_op jit(solution)/shard_map/ppermute | solution.py:14
  45.2 75.4 %collective-permute-start.11 = (bf16[18,1,4,64]{3,2,1,0:T(4,128)(2,1)}, bf16[18,1,4,64]{3,2,1,0:T(4,128)(2,1)}, u32[]{:S(2)}, u32[]{:S(2)}) collective-permute-start(bf16[18,1,4,64]{3,2,1,0:T(4,128)(2,1)} %get-tuple-element.490), channel_id=1, source_target_pairs={{1,0},{2,1},{3,2},{4,3},{5,4},{6,5},{7,6},{8,7},{9,8},{10,9},{11,1... | collective-permute-start | bytes 27656 | tf_op jit(solution)/shard_map/ppermute | solution.py:17
  119.8 0.8 copy-start.2
  220.1 2.3 copy-start.14
  220.1 3.1 copy-start.3
  220.1 3.1 copy-start.4
  224.4 33.0 %collective-permute-start.4 = (bf16[1,16,4,64]{3,2,1,0:T(4,128)(2,1)S(1)}, bf16[1,16,4,64]{3,2,1,0:T(4,128)(2,1)S(1)}, u32[]{:S(2)}, u32[]{:S(2)}) collective-permute-start(bf16[1,16,4,64]{3,2,1,0:T(4,128)(2,1)S(1)} %get-tuple-element.497), channel_id=1, source_target_pairs={{0,16},{16,32},{32,48},{48,64},{64,80},{80,96},{96,112},{112,128},... | collective-permute-start | bytes 24584 | tf_op jit(solution)/shard_map/ppermute | solution.py:14
  228.7 28.8 %collective-permute-start.5 = (bf16[1,16,4,64]{3,2,1,0:T(4,128)(2,1)S(1)}, bf16[1,16,4,64]{3,2,1,0:T(4,128)(2,1)S(1)}, u32[]{:S(2)}, u32[]{:S(2)}) collective-permute-start(bf16[1,16,4,64]{3,2,1,0:T(4,128)(2,1)S(1)} %get-tuple-element.498), channel_id=1, source_target_pairs={{16,0},{32,16},{48,32},{64,48},{80,64},{96,80},{112,96},{128,112},... | collective-permute-start | bytes 24584 | tf_op jit(solution)/shard_map/ppermute | solution.py:17
  230.6 25.1 %copy-start.16 = (pred[256]{0:T(512)(128)(4,1)S(1)}, pred[256]{0:T(512)(128)(4,1)}, u32[]{:S(2)}) copy-start(pred[256]{0:T(512)(128)(4,1)} %copy-done.15) | copy-start | bytes 772
  255.6 1.0 copy-start.7
  257.5 9.9 %collective-permute-start.6 = (bf16[18,1,4,64]{3,2,1,0:T(4,128)(2,1)S(1)}, bf16[18,1,4,64]{3,2,1,0:T(4,128)(2,1)S(1)}, u32[]{:S(2)}, u32[]{:S(2)}) collective-permute-start(bf16[18,1,4,64]{3,2,1,0:T(4,128)(2,1)S(1)} %get-tuple-element.491), channel_id=1, source_target_pairs={{0,1},{1,2},{2,3},{3,4},{4,5},{5,6},{6,7},{7,8},{8,9},{9,10},{10,1... | collective-permute-start | bytes 27656 | tf_op jit(solution)/shard_map/ppermute | solution.py:14
  263.3 6.9 collective-permute-start.7
  267.4 390.6 %all-reduce.12.cloned.1.call-start = ((), (), s32[]{:S(2)}) async-start(), calls=%async_computation.1 | async-start | bytes 262144 | tf_op jit(solution)/shard_map/psum | solution.py:96
  438.6 502.8 %all-reduce.10.cloned.1.call-start = ((), (), s32[]{:S(2)}) async-start(), calls=%async_computation | async-start | bytes 3538944 | tf_op jit(solution)/shard_map/psum | solution.py:124
  658.0 9.4 copy-start.11
  658.0 10.8 %copy-start.9 = (f32[64,64]{1,0:T(8,128)S(1)}, f32[64,64]{1,0:T(8,128)}, u32[]{:S(2)}) copy-start(f32[64,64]{1,0:T(8,128)} %get-tuple-element.340) | copy-start | bytes 49156
  658.0 10.8 %copy-start.10 = (f32[64,64]{1,0:T(8,128)S(1)}, f32[64,64]{1,0:T(8,128)}, u32[]{:S(2)}) copy-start(f32[64,64]{1,0:T(8,128)} %get-tuple-element.341) | copy-start | bytes 49156
  945.7 1.2 copy-start.8
Sparse Core Ops, SparseCore 0:
  267.5 171.0 all-reduce.13
  442.1 215.8 all-reduce.11
  663.1 278.2 all-reduce.9
